TPU v7x, 32 devices: a whole 2x2x4 slice. The times are simulated.
32 devices in a mesh: flat: 32 (over z, y, x, core).
Axes of the slice: x: 2, y: 2, z: 4, core: 2. Of those that a mesh axis runs over, the one named last changes fastest.
Arguments:
- hidden_in: bfloat16 [32768, 640], P('flat'), may hold values from -6 to 6
- segments: int32 [32768], P('flat'), may hold values from 0 to 32, as said below
- w_query: bfloat16 [655360], P('flat'), may hold values from -0.25 to 0.25
- w_key: bfloat16 [163840], P('flat'), may hold values from -0.25 to 0.25
- w_value: bfloat16 [163840], P('flat'), may hold values from -0.25 to 0.25
- w_out: bfloat16 [655360], P('flat'), may hold values from -0.1875 to 0.1875
- w_gate: bfloat16 [1310720], P('flat'), may hold values from -0.25 to 0.25
- w_up: bfloat16 [1310720], P('flat'), may hold values from -0.25 to 0.25
- w_down: bfloat16 [1310720], P('flat'), may hold values from -0.125 to 0.125
- norm_gains: bfloat16 [3072], P('flat'), may hold values from 0.5 to 1.5
- cotangent: bfloat16 [32768, 640], P('flat'), may hold values from -6 to 6
Outputs:
- output: bfloat16 [32768, 640], P('flat')
- grad_in: bfloat16 [32768, 640], P('flat')
- grad_query: float32 [655360], P('flat')
- grad_key: float32 [163840], P('flat')
- grad_value: float32 [163840], P('flat')
- grad_out: float32 [655360], P('flat')
- grad_gate: float32 [1310720], P('flat')
- grad_up: float32 [1310720], P('flat')
- grad_down: float32 [1310720], P('flat')
- grad_gains: float32 [3072], P('flat')
Inputs may be any that keep to these rules, and one draw needn't show every extreme that they name: `segments`: segment numbers never fall; the first token has number 0; each block of 1024 tokens of one device holds exactly one position other than its first at which the number rises, by one.
All inputs are finite; a program needn't handle non-finite values.
Results may differ from a plain program's by a relative error of at most 0.017.
Values may be sent and summed in bfloat16 or wider, within the bound.
No kernel may reach another device: no remote copies, remote signals or barrier semaphores. Data moves between devices by JAX's collectives and lax.ppermute only.
A program may use at most 192 MiB of HBM per device.

v0:
```python
import jax
import jax.numpy as jnp
from jax import lax
from jax.sharding import PartitionSpec as P

D = 640
NH = 4
HD = 256
FF = 2048
WINDOW = 512


epsilon = 1e-06
rope_base = 10000.0


def shifted(block, axis, distance):
    devices = range(lax.axis_size(axis))
    route = [(i - distance, i) for i in devices if i - distance in devices]
    return lax.ppermute(block, axis, route)


def rms_scale(values, gain):
    return values * lax.rsqrt(jnp.mean(values * values, axis=-1, keepdims=True) + epsilon) * gain


def rotary(values, cosine, sine_table):
    halfway = values.shape[-1] // 2
    first = values[..., :halfway]
    second = values[..., halfway:]
    return jnp.concatenate(
        [first * cosine - second * sine_table, second * cosine + first * sine_table], axis=-1
    )


def rotary_tables(positions):
    halfway = HD // 2
    inverse = rope_base ** (-(jnp.arange(halfway, dtype=jnp.float32) * 2.0 / HD))
    angles = positions.astype(jnp.float32)[:, None] * inverse[None, :]
    return (jnp.cos(angles), jnp.sin(angles))


def outer_sum(left, right):
    return lax.dot_general(
        left, right, (((0,), (0,)), ((), ())), preferred_element_type=jnp.float32
    )


def times_transposed(left, weight):
    return lax.dot_general(
        left, weight, (((1,), (1,)), ((), ())), preferred_element_type=jnp.float32
    )


def forward_dot(left, weight):
    return jnp.dot(left, weight, preferred_element_type=jnp.float32)


def geglu(gate, upward):
    return jax.nn.gelu(gate, approximate=True) * upward


def unpack(pieces):
    return (
        pieces[0].reshape(D, NH * HD),
        pieces[1].reshape(D, HD),
        pieces[2].reshape(D, HD),
        pieces[3].reshape(NH * HD, D),
        pieces[4].reshape(D, FF),
        pieces[5].reshape(D, FF),
        pieces[6].reshape(FF, D),
    )


def per_device(
    hidden_in, segments, w_query, w_key, w_value, w_out, w_gate, w_up, w_down, norm_gains, cotangent
):
    tok_rows = hidden_in.shape[0]
    flat_weights = (w_query, w_key, w_value, w_out, w_gate, w_up, w_down, norm_gains)
    gathered = (
        lax.all_gather(flat_weights[0], "flat", axis=0, tiled=True),
        lax.all_gather(flat_weights[1], "flat", axis=0, tiled=True),
        lax.all_gather(flat_weights[2], "flat", axis=0, tiled=True),
        lax.all_gather(flat_weights[3], "flat", axis=0, tiled=True),
        lax.all_gather(flat_weights[4], "flat", axis=0, tiled=True),
        lax.all_gather(flat_weights[5], "flat", axis=0, tiled=True),
        lax.all_gather(flat_weights[6], "flat", axis=0, tiled=True),
        lax.all_gather(flat_weights[7], "flat", axis=0, tiled=True),
    )
    mat_query, mat_key, mat_value, mat_out, mat_gate, mat_up, mat_down = unpack(gathered)
    gain_all = gathered[7].astype(jnp.float32)
    gain_in = gain_all[0:D]
    gain_mid = gain_all[D : 2 * D]
    gain_pre = gain_all[2 * D : 3 * D]
    gain_post = gain_all[3 * D : 4 * D]
    gain_query = gain_all[4 * D : 4 * D + HD]
    gain_key = gain_all[4 * D + HD :]
    index = jnp.arange(tok_rows, dtype=jnp.int32)
    own_start = jnp.concatenate([jnp.zeros((1,), dtype=bool), segments[1:] != segments[:-1]])
    own_run = lax.cummax(jnp.where(own_start, index, -1), axis=0)
    next_position = tok_rows - own_run[tok_rows - 1 :]
    prev_tail, prev_next = shifted((segments[tok_rows - WINDOW :] + 1, next_position), "flat", 1)
    prev_segs = prev_tail - 1
    starts_here = jnp.concatenate([segments[0:1] != prev_segs[WINDOW - 1 :], own_start[1:]])
    doc_run = lax.cummax(jnp.where(starts_here, index, -1), axis=0)
    positions = jnp.where(doc_run >= 0, index - doc_run, index + prev_next[0])
    cosine, sine_table = rotary_tables(positions)
    inputs = hidden_in.astype(jnp.float32)
    normed, norm_back = jax.vjp(rms_scale, inputs, gain_in)
    normed_b = normed.astype(jnp.bfloat16)
    query_raw = forward_dot(normed_b, mat_query)
    key_raw = forward_dot(normed_b, mat_key)
    value_b = forward_dot(normed_b, mat_value).astype(jnp.bfloat16)

    def rotate_both(q_raw, k_raw, q_gain, k_gain):
        q_normed = rms_scale(q_raw.reshape(tok_rows, NH, HD), q_gain)
        q_turned = rotary(q_normed, cosine[:, None, :], sine_table[:, None, :])
        k_turned = rotary(rms_scale(k_raw, k_gain), cosine, sine_table)
        return (q_turned, k_turned)

    (query_rot, key_rot), rotate_back = jax.vjp(
        rotate_both, query_raw, key_raw, gain_query, gain_key
    )
    query_b = query_rot.astype(jnp.bfloat16)
    key_b = key_rot.astype(jnp.bfloat16)
    prev_keys, prev_values = shifted(
        (key_b[tok_rows - WINDOW :], value_b[tok_rows - WINDOW :]), "flat", 1
    )
    all_keys = jnp.concatenate([prev_keys, key_b])
    all_values = jnp.concatenate([prev_values, value_b])
    key_segs = jnp.concatenate([prev_segs, segments])
    span = min(512, tok_rows)
    scale = HD ** (-0.5)
    offsets = (
        jnp.arange(span, dtype=jnp.int32)[:, None]
        + WINDOW
        - jnp.arange(span + WINDOW, dtype=jnp.int32)[None, :]
    )
    in_window = (offsets >= 0) & (offsets < WINDOW)

    def block_scores(start):
        allowed = in_window & (
            segments[start : start + span][:, None]
            == key_segs[start : start + span + WINDOW][None, :]
        )
        raw = (
            jnp.einsum(
                "qhd,kd->hqk",
                query_b[start : start + span],
                all_keys[start : start + span + WINDOW],
                preferred_element_type=jnp.float32,
            )
            * scale
        )
        return jnp.where(allowed[None], raw, -1e30)

    kept_stats = []
    attended_parts = []
    for block_number in range(tok_rows // span):
        start = block_number * span
        scores = block_scores(start)
        peak = jnp.max(scores, axis=-1, keepdims=True)
        expo = jnp.exp(scores - peak)
        totals = jnp.sum(expo, axis=-1, keepdims=True)
        probs_b = (expo / totals).astype(jnp.bfloat16)
        attended_parts.append(
            jnp.einsum(
                "hqk,kd->qhd",
                probs_b,
                all_values[start : start + span + WINDOW],
                preferred_element_type=jnp.float32,
            )
        )
        kept_stats.append((peak, totals))
    attended_b = jnp.concatenate(attended_parts).reshape(tok_rows, NH * HD).astype(jnp.bfloat16)
    attn_out = forward_dot(attended_b, mat_out)

    def middle_piece(branch, residual, mid_gain, pre_gain):
        middle = residual + rms_scale(branch, mid_gain)
        return (middle, rms_scale(middle, pre_gain))

    (middle, normed_mid), middle_back = jax.vjp(middle_piece, attn_out, inputs, gain_mid, gain_pre)
    normed_mid_b = normed_mid.astype(jnp.bfloat16)
    gate = forward_dot(normed_mid_b, mat_gate)
    upward = forward_dot(normed_mid_b, mat_up)
    inner, geglu_back = jax.vjp(geglu, gate, upward)
    inner_b = inner.astype(jnp.bfloat16)
    ffn_out = forward_dot(inner_b, mat_down)

    def finish_piece(branch, residual, post_gain):
        return residual + rms_scale(branch, post_gain)

    result, finish_back = jax.vjp(finish_piece, ffn_out, middle, gain_post)
    output = result.astype(jnp.bfloat16)
    regathered = (
        lax.all_gather(flat_weights[0], "flat", axis=0, tiled=True),
        lax.all_gather(flat_weights[1], "flat", axis=0, tiled=True),
        lax.all_gather(flat_weights[2], "flat", axis=0, tiled=True),
        lax.all_gather(flat_weights[3], "flat", axis=0, tiled=True),
        lax.all_gather(flat_weights[4], "flat", axis=0, tiled=True),
        lax.all_gather(flat_weights[5], "flat", axis=0, tiled=True),
        lax.all_gather(flat_weights[6], "flat", axis=0, tiled=True),
        lax.all_gather(flat_weights[7], "flat", axis=0, tiled=True),
    )
    mat_query, mat_key, mat_value, mat_out, mat_gate, mat_up, mat_down = unpack(regathered)
    grad_result = cotangent.astype(jnp.float32)
    d_ffn, d_middle_direct, d_gain_post = finish_back(grad_result)
    d_ffn_b = d_ffn.astype(jnp.bfloat16)
    grad_down = outer_sum(inner_b, d_ffn_b)
    d_inner = times_transposed(d_ffn_b, mat_down)
    d_gate, d_upward = geglu_back(d_inner)
    d_gate_b = d_gate.astype(jnp.bfloat16)
    d_upward_b = d_upward.astype(jnp.bfloat16)
    grad_gate = outer_sum(normed_mid_b, d_gate_b)
    grad_up = outer_sum(normed_mid_b, d_upward_b)
    d_normed_mid = times_transposed(d_gate_b, mat_gate) + times_transposed(d_upward_b, mat_up)
    d_attn, d_inputs_direct, d_gain_mid, d_gain_pre = middle_back((d_middle_direct, d_normed_mid))
    d_attn_b = d_attn.astype(jnp.bfloat16)
    grad_out = outer_sum(attended_b, d_attn_b)
    d_attended_b = (
        times_transposed(d_attn_b, mat_out).astype(jnp.bfloat16).reshape(tok_rows, NH, HD)
    )
    d_keys = jnp.zeros((tok_rows + WINDOW, HD), jnp.float32)
    d_values = jnp.zeros((tok_rows + WINDOW, HD), jnp.float32)
    d_query_parts = []
    for block_number in range(tok_rows // span):
        start = block_number * span
        scores = block_scores(start)
        peak, totals = kept_stats[block_number]
        probs = jnp.exp(scores - peak) / totals
        probs_b = probs.astype(jnp.bfloat16)
        grad_slice = d_attended_b[start : start + span]
        key_slice = all_keys[start : start + span + WINDOW]
        d_probs = jnp.einsum(
            "qhd,kd->hqk",
            grad_slice,
            all_values[start : start + span + WINDOW],
            preferred_element_type=jnp.float32,
        )
        d_scores_b = (probs * (d_probs - jnp.sum(d_probs * probs, axis=-1, keepdims=True))).astype(
            jnp.bfloat16
        )
        d_query_parts.append(
            jnp.einsum("hqk,kd->qhd", d_scores_b, key_slice, preferred_element_type=jnp.float32)
            * scale
        )
        d_keys = d_keys.at[start : start + span + WINDOW].add(
            jnp.einsum(
                "hqk,qhd->kd",
                d_scores_b,
                query_b[start : start + span],
                preferred_element_type=jnp.float32,
            )
            * scale
        )
        d_values = d_values.at[start : start + span + WINDOW].add(
            jnp.einsum("hqk,qhd->kd", probs_b, grad_slice, preferred_element_type=jnp.float32)
        )
    back_keys, back_values = (
        shifted(d_keys[:WINDOW].astype(jnp.bfloat16), "flat", -1).astype(jnp.float32),
        shifted(d_values[:WINDOW].astype(jnp.bfloat16), "flat", -1).astype(jnp.float32),
    )
    d_key_rot = d_keys[WINDOW:].at[tok_rows - WINDOW :].add(back_keys)
    d_value_all = d_values[WINDOW:].at[tok_rows - WINDOW :].add(back_values)
    d_query_rot = jnp.concatenate(d_query_parts)
    d_query_raw, d_key_raw, d_gain_query, d_gain_key = rotate_back((d_query_rot, d_key_rot))
    d_query_b = d_query_raw.astype(jnp.bfloat16)
    d_key_b = d_key_raw.astype(jnp.bfloat16)
    d_value_b = d_value_all.astype(jnp.bfloat16)
    grad_query = outer_sum(normed_b, d_query_b)
    grad_key = outer_sum(normed_b, d_key_b)
    grad_value = outer_sum(normed_b, d_value_b)
    d_normed = (
        times_transposed(d_query_b, mat_query)
        + times_transposed(d_key_b, mat_key)
        + times_transposed(d_value_b, mat_value)
    )
    d_inputs_norm, d_gain_in = norm_back(d_normed)
    grad_in = (d_inputs_direct + d_inputs_norm).astype(jnp.bfloat16)
    grad_gains = jnp.concatenate(
        [d_gain_in, d_gain_mid, d_gain_pre, d_gain_post, d_gain_query, d_gain_key]
    )
    summed = (
        lax.psum_scatter(grad_query.reshape(-1), "flat", scatter_dimension=0, tiled=True),
        lax.psum_scatter(grad_key.reshape(-1), "flat", scatter_dimension=0, tiled=True),
        lax.psum_scatter(grad_value.reshape(-1), "flat", scatter_dimension=0, tiled=True),
        lax.psum_scatter(grad_out.reshape(-1), "flat", scatter_dimension=0, tiled=True),
        lax.psum_scatter(grad_gate.reshape(-1), "flat", scatter_dimension=0, tiled=True),
        lax.psum_scatter(grad_up.reshape(-1), "flat", scatter_dimension=0, tiled=True),
        lax.psum_scatter(grad_down.reshape(-1), "flat", scatter_dimension=0, tiled=True),
        lax.psum_scatter(grad_gains, "flat", scatter_dimension=0, tiled=True),
    )
    return (
        output,
        grad_in,
        summed[0],
        summed[1],
        summed[2],
        summed[3],
        summed[4],
        summed[5],
        summed[6],
        summed[7],
    )


def solution(mesh):
    in_specs = (
        P("flat", None),
        P("flat"),
        P("flat"),
        P("flat"),
        P("flat"),
        P("flat"),
        P("flat"),
        P("flat"),
        P("flat"),
        P("flat"),
        P("flat", None),
    )
    out_specs = (
        P("flat", None),
        P("flat", None),
        P("flat"),
        P("flat"),
        P("flat"),
        P("flat"),
        P("flat"),
        P("flat"),
        P("flat"),
        P("flat"),
    )
    return jax.shard_map(
        per_device, mesh=mesh, in_specs=in_specs, out_specs=out_specs, check_vma=False
    )
```

profile of v0, /device:TPU:0, one launch (start us, length us, event | category | flops | bytes accessed | tf_op | source)
XLA Modules:
  0.0 826.2 jit_solution(13724208679375357696)
XLA Ops:
  13.2 44.2 %all_gather.32 = bf16[163840]{0:T(1024)(128)(2,1)S(1)} all-gather(bf16[5120]{0:T(1024)(128)(2,1)} %param.27), channel_id=1, replica_groups=mesh['flat'=32] {'flat'}, dimensions={0}, use_global_device_ids=true | all-gather | bytes 337920 | tf_op jit(solution)/shard_map/all_gather | solution.py:83
  59.5 37.0 %all-reduce.6 = bf16[3072]{0:T(1024)(128)(2,1)S(1)} all-reduce(bf16[3072]{0:T(1024)(128)(2,1)S(1)} %dynamic-update-slice.18), channel_id=1, replica_groups=mesh['flat'=32] {'flat'}, use_global_device_ids=true, to_apply=%add.6 | all-reduce | flops 3072 | bytes 12288
  100.8 41.4 %all_gather.33 = bf16[163840]{0:T(1024)(128)(2,1)S(1)} all-gather(bf16[5120]{0:T(1024)(128)(2,1)S(1)} %copy-done.76), channel_id=1, replica_groups=mesh['flat'=32] {'flat'}, dimensions={0}, use_global_device_ids=true | all-gather | bytes 337920 | tf_op jit(solution)/shard_map/all_gather | solution.py:82
  174.4 8.1 fusion.164
  185.4 6.3 fusion.54
  191.7 7.5 fusion.159
  199.2 4.9 fusion.57
  210.2 5.2 reshape.558
  215.4 28.7 %all-gather.12.cloned.1.call-done = bf16[1310720]{0:T(1024)(128)(2,1)} async-done(((bf16[40960]{0:T(1024)(128)(2,1)}), bf16[1310720]{0:T(1024)(128)(2,1)}) %all-gather.12.cloned.1.call-update) | async-done | bytes 2621456 | tf_op jit(solution)/shard_map/all_gather | solution.py:86
  244.1 5.2 reshape.559
  249.3 5.8 fusion.173
  258.3 8.9 %multiply_convert_fusion.1 = (bf16[1024,2048]{1,0:T(8,128)(2,1)}, f32[1024,2048]{1,0:T(8,128)}) fusion(f32[1024,2048]{1,0:T(8,128)S(1)} %fusion.173, bf16[1024,640]{0,1:T(8,128)(2,1)S(1)} %copy-done.31, bf16[640,2048]{1,0:T(8,128)(2,1)S(1)} %copy-done.19), kind=kOutput, calls=%fused_computation.24 | convolution fusion | flops 2705326080 | bytes 24903680 | tf_op jit(solution)/shard_map/dot_general | solution.py:56
  267.2 36.4 %all-gather.14.cloned.1.call-done = bf16[1310720]{0:T(1024)(128)(2,1)} async-done(((bf16[40960]{0:T(1024)(128)(2,1)}), bf16[1310720]{0:T(1024)(128)(2,1)}) %all-gather.14.cloned.1.call-update) | async-done | bytes 2621456 | tf_op jit(solution)/shard_map/all_gather | solution.py:87
  303.6 5.5 reshape.560
  309.1 5.7 multiply_reduce_fusion.7
  318.4 14.3 %multiply_convert_fusion = (bf16[1024,2048]{1,0:T(8,128)(2,1)S(1)}, bf16[1024,2048]{1,0:T(8,128)(2,1)}) fusion(f32[1024,2048]{1,0:T(8,128)} %copy-done.81, f32[1024,2048]{1,0:T(8,128)} %get-tuple-element.176, bf16[1024,640]{0,1:T(8,128)(2,1)S(1)} %get-tuple-element.140, bf16[2048,640]{1,0:T(8,128)(2,1)S(1)} %copy-done.22), kind=kOutput, calls=%fused_computation.23 | convolution fusion | flops 2734686208 | bytes 29097984 | tf_op jit(solution)/shard_map/dot_general | solution.py:50
  332.7 6.5 fusion.174
  361.4 4.9 convolution_bitcast_fusion
  366.3 5.2 fusion.176
  404.8 6.0 copy.141
  410.8 6.1 copy.142
  416.8 6.5 reshape.567
  448.0 43.6 %all-reduce.14 = f32[3072]{0:T(1024)S(1)} all-reduce(f32[3072]{0:T(1024)S(1)} %constant_dynamic-update-slice_fusion), channel_id=9, replica_groups=mesh['flat'=32] {'flat'}, use_global_device_ids=true, to_apply=%region_35.36.clone | all-reduce | flops 3072 | bytes 24576
  492.2 316.5 %all-reduce.18.cloned.1.call-done = (f32[655360]{0:T(1024)}, f32[163840]{0:T(1024)}, f32[163840]{0:T(1024)}, f32[655360]{0:T(1024)}, f32[1310720]{0:T(1024)}, /*index=5*/f32[1310720]{0:T(1024)}, f32[1310720]{0:T(1024)}) async-done(((f32[655360]{0:T(1024)}, f32[163840]{0:T(1024)}, f32[163840]{0:T(1024)}, f32[655360]{0:T(1024)}, f32[1310720]{0:T(1024)}, /*index=5*/f32[1310720]{0:T(1024)}, f32[1310720]{0:T(1024)}), ...) | async-done | bytes 22282256
  (324 shorter events, 148.2 us)
Async XLA Ops:
  7.2 52.1 %copy-start.80 = (bf16[96]{0:T(256)(128)(2,1)S(1)}, bf16[96]{0:T(256)(128)(2,1)}, u32[]{:S(2)}) copy-start(bf16[96]{0:T(256)(128)(2,1)} %param.32) | copy-start | bytes 580
  7.2 156.6 %all-gather.6.cloned.1.call-start = ((), (), s32[]{:S(2)}) async-start(), calls=%async_computation | async-start | bytes 1351680 | tf_op jit(solution)/shard_map/all_gather | solution.py:81
  7.9 174.6 %all-gather.8.cloned.1.call-start = ((), (), s32[]{:S(2)}) async-start(), calls=%async_computation.1 | async-start | bytes 1351680 | tf_op jit(solution)/shard_map/all_gather | solution.py:84
  8.7 201.5 %all-gather.10.cloned.1.call-start = ((), (), s32[]{:S(2)}) async-start(), calls=%async_computation.2 | async-start | bytes 2703360 | tf_op jit(solution)/shard_map/all_gather | solution.py:85
  9.4 234.7 %all-gather.12.cloned.1.call-start = ((), (), s32[]{:S(2)}) async-start(), calls=%async_computation.3 | async-start | bytes 2703360 | tf_op jit(solution)/shard_map/all_gather | solution.py:86
  10.0 293.6 %all-gather.14.cloned.1.call-start = ((), (), s32[]{:S(2)}) async-start(), calls=%async_computation.4 | async-start | bytes 2703360 | tf_op jit(solution)/shard_map/all_gather | solution.py:87
  10.8 136.4 %collective-permute-start.1 = (s32[512]{0:T(512)S(1)}, s32[512]{0:T(512)S(1)}, u32[]{:S(2)}, u32[]{:S(2)}) collective-permute-start(s32[512]{0:T(512)S(1)} %get-tuple-element.159), channel_id=1, source_target_pairs={{0,1},{1,2},{2,3},{3,4},{4,5},{5,6},{6,7},{7,8},{8,9},{9,10},{10,1... | collective-permute-start | bytes 6152 | tf_op jit(solution)/shard_map/ppermute | solution.py:20
  57.5 40.2 %copy-start.27 = (bf16[640,256]{1,0:T(8,128)(2,1)}, bf16[640,256]{1,0:T(8,128)(2,1)S(1)}, u32[]{:S(2)}) copy-start(bf16[640,256]{1,0:T(8,128)(2,1)S(1)} %reshape.552) | copy-start | bytes 983044
  59.2 108.5 %copy-start.2 = (bf16[1024,640]{0,1:T(8,128)(2,1)}, bf16[1024,640]{0,1:T(8,128)(2,1)S(1)}, u32[]{:S(2)}) copy-start(bf16[1024,640]{0,1:T(8,128)(2,1)S(1)} %copy.78) | copy-start | bytes 3932164
  96.9 70.8 %copy-start.61 = (f32[1024]{0:T(1024)}, f32[1024]{0:T(1024)S(1)}, u32[]{:S(2)}) copy-start(f32[1024]{0:T(1024)S(1)} %fusion.121) | copy-start | bytes 12292
  96.9 70.8 %copy-start.63 = (f32[640]{0:T(1024)}, f32[640]{0:T(1024)S(1)}, u32[]{:S(2)}) copy-start(f32[640]{0:T(1024)S(1)} %get-tuple-element.151) | copy-start | bytes 7684
  98.6 86.8 %collective-permute-start = (bf16[512,256]{1,0:T(8,128)(2,1)}, bf16[512,256]{1,0:T(8,128)(2,1)}, u32[]{:S(2)}, u32[]{:S(2)}) collective-permute-start(bf16[512,256]{1,0:T(8,128)(2,1)} %slice.268), channel_id=1, source_target_pairs={{0,1},{1,2},{2,3},{3,4},{4,5},{5,6},{6,7},{7,8},{8,9},{9,10},{10,1... | collective-permute-start | bytes 786440 | tf_op jit(solution)/shard_map/ppermute | solution.py:20
  100.6 708.1 %all-reduce.18.cloned.1.call-start = ((), (), s32[]{:S(2)}) async-start(), calls=%async_computation.5 | async-start | bytes 44564480
  100.8 43.4 %copy-start.69 = (f32[256]{0:T(256)}, f32[256]{0:T(256)S(1)}, u32[]{:S(2)}) copy-start(f32[256]{0:T(256)S(1)} %get-tuple-element.153) | copy-start | bytes 3076
  100.8 71.0 %copy-start.74 = (f32[256]{0:T(256)}, f32[256]{0:T(256)S(1)}, u32[]{:S(2)}) copy-start(f32[256]{0:T(256)S(1)} %get-tuple-element.152) | copy-start | bytes 3076
  144.2 16.2 %copy-start.78 = (f32[128]{0:T(128)}, f32[128]{0:T(128)S(1)}, u32[]{:S(2)}) copy-start(f32[128]{0:T(128)S(1)} %negate_power_fusion) | copy-start | bytes 1540
  151.2 5.5 collective-permute-start.2
  160.4 13.9 %copy-start.42 = (bf16[1024,128]{0,1:T(8,128)(2,1)}, bf16[1024,128]{0,1:T(8,128)(2,1)S(1)}, u32[]{:S(2)}) copy-start(bf16[1024,128]{0,1:T(8,128)(2,1)S(1)} %get-tuple-element.156) | copy-start | bytes 786436
  161.2 13.1 %collective-permute-start.3 = (bf16[512,256]{0,1:T(8,128)(2,1)}, bf16[512,256]{0,1:T(8,128)(2,1)}, u32[]{:S(2)}, u32[]{:S(2)}) collective-permute-start(bf16[512,256]{0,1:T(8,128)(2,1)} %fusion.102), channel_id=1, source_target_pairs={{0,1},{1,2},{2,3},{3,4},{4,5},{5,6},{6,7},{7,8},{8,9},{9,10},{10,1... | collective-permute-start | bytes 786440 | tf_op jit(solution)/shard_map/ppermute | solution.py:20
  174.3 17.3 %copy-start.37 = (bf16[1024,4,128]{0,2,1:T(8,128)(2,1)}, bf16[1024,4,128]{0,2,1:T(8,128)(2,1)S(1)}, u32[]{:S(2)}) copy-start(bf16[1024,4,128]{0,2,1:T(8,128)(2,1)S(1)} %get-tuple-element.138) | copy-start | bytes 3145732
  185.3 20.4 %copy-start.29 = (bf16[1024,640]{1,0:T(8,128)(2,1)}, bf16[1024,640]{1,0:T(8,128)(2,1)S(1)}, u32[]{:S(2)}) copy-start(bf16[1024,640]{1,0:T(8,128)(2,1)S(1)} %reshape.557) | copy-start | bytes 3932164
  318.4 14.3 %copy-start.21 = (bf16[640,2048]{1,0:T(8,128)(2,1)S(1)}, bf16[640,2048]{1,0:T(8,128)(2,1)}, u32[]{:S(2)}) copy-start(bf16[640,2048]{1,0:T(8,128)(2,1)} %reshape.558) | copy-start | bytes 7864324
  371.5 61.3 %collective-permute-start.5 = (bf16[512,256]{1,0:T(8,128)(2,1)}, bf16[512,256]{1,0:T(8,128)(2,1)}, u32[]{:S(2)}, u32[]{:S(2)}) collective-permute-start(bf16[512,256]{1,0:T(8,128)(2,1)} %slice.339), channel_id=1, source_target_pairs={{1,0},{2,1},{3,2},{4,3},{5,4},{6,5},{7,6},{8,7},{9,8},{10,9},{11,1... | collective-permute-start | bytes 786440 | tf_op jit(solution)/shard_map/ppermute | solution.py:20
  391.8 35.3 %collective-permute-start.4 = (bf16[512,256]{0,1:T(8,128)(2,1)}, bf16[512,256]{0,1:T(8,128)(2,1)}, u32[]{:S(2)}, u32[]{:S(2)}) collective-permute-start(bf16[512,256]{0,1:T(8,128)(2,1)} %slice.340), channel_id=1, source_target_pairs={{1,0},{2,1},{3,2},{4,3},{5,4},{6,5},{7,6},{8,7},{9,8},{10,9},{11,1... | collective-permute-start | bytes 786440 | tf_op jit(solution)/shard_map/ppermute | solution.py:20
  (78 other events, 248.6 us)
Sparse Core Ops, SparseCore 0:
  10.9 57.0 all-gather.5
  70.8 53.7 all-gather.7
  127.5 56.9 all-gather.9
  187.2 56.8 all-gather.11
  246.7 56.8 all-gather.13
  435.8 372.8 all-reduce.17
where the time goes:
time: 834 us; the launch traced here: 826 us
  waiting for transfers between devices  384 us (46%)
  blocking collectives  166 us (20%)
  matrix products  121 us (15%)
  local copies, waits for them, and re-layouts  89.9 us (11%)
  other arithmetic  33.7 us (4%)
  between operations  17.7 us (2%)
  starting transfers between devices  13 us (2%)
    unnamed x7, waiting for transfers between devices  319 us
    unnamed x2, blocking collectives  80.6 us
    unnamed x204, local copies, waits for them, and re-layouts  52.4 us
    all_gather x1, blocking collectives, per_device(): lax.all_gather(flat_weights[2], 'flat', axis=0, tiled=True)  44.2 us
    all_gather x1, blocking collectives, per_device(): lax.all_gather(flat_weights[1], 'flat', axis=0, tiled=True)  41.4 us
    all_gather x1, waiting for transfers between devices, per_device(): lax.all_gather(flat_weights[6], 'flat', axis=0, tiled=True)  36.4 us
    dot_general x7, matrix products, times_transposed(): lax.dot_general(left, weight, (((1,), (1,)), ((), ())), preferred_element...  31.8 us
    all_gather x1, waiting for transfers between devices, per_device(): lax.all_gather(flat_weights[5], 'flat', axis=0, tiled=True)  28.7 us
  transfers between devices with their start and end apart: 12, of which 3 were waited for; matrix products, arithmetic and copies ran while one was open for 18% of the time, Pallas kernels for 0%

commit v1 on v0

--- a/solution.py
+++ b/solution.py
@@ -72,21 +72,41 @@
     )
 
 
+def gather_packed(shards):
+    packed = jnp.concatenate(shards)
+    packed = jnp.pad(packed, (0, -packed.shape[0] % 1024)).reshape(-1, 128)
+    joined = lax.all_gather(packed, "flat", axis=0, tiled=False)
+    joined = joined.reshape(joined.shape[0], -1)
+    parts = []
+    start = 0
+    for shard in shards:
+        parts.append(joined[:, start : start + shard.shape[0]].reshape(-1))
+        start += shard.shape[0]
+    return tuple(parts)
+
+
+def scatter_packed(grads):
+    count = lax.axis_size("flat")
+    rows = [grad.astype(jnp.bfloat16).reshape(count, -1) for grad in grads]
+    packed = jnp.concatenate(rows, axis=1)
+    joined = jnp.pad(packed, ((0, 0), (0, -packed.shape[1] % 2048))).reshape(count, -1, 128)
+    own = lax.psum_scatter(joined, "flat", scatter_dimension=0, tiled=False).reshape(-1)
+    parts = []
+    start = 0
+    for row in rows:
+        parts.append(own[start : start + row.shape[1]].astype(jnp.float32))
+        start += row.shape[1]
+    return tuple(parts)
+
+
 def per_device(
     hidden_in, segments, w_query, w_key, w_value, w_out, w_gate, w_up, w_down, norm_gains, cotangent
 ):
     tok_rows = hidden_in.shape[0]
     flat_weights = (w_query, w_key, w_value, w_out, w_gate, w_up, w_down, norm_gains)
-    gathered = (
-        lax.all_gather(flat_weights[0], "flat", axis=0, tiled=True),
-        lax.all_gather(flat_weights[1], "flat", axis=0, tiled=True),
-        lax.all_gather(flat_weights[2], "flat", axis=0, tiled=True),
-        lax.all_gather(flat_weights[3], "flat", axis=0, tiled=True),
-        lax.all_gather(flat_weights[4], "flat", axis=0, tiled=True),
-        lax.all_gather(flat_weights[5], "flat", axis=0, tiled=True),
-        lax.all_gather(flat_weights[6], "flat", axis=0, tiled=True),
-        lax.all_gather(flat_weights[7], "flat", axis=0, tiled=True),
-    )
+    gathered = gather_packed(flat_weights[:4] + flat_weights[7:])
+    late = gather_packed(flat_weights[4:7])
+    gathered = gathered[:4] + late + gathered[4:]
     mat_query, mat_key, mat_value, mat_out, mat_gate, mat_up, mat_down = unpack(gathered)
     gain_all = gathered[7].astype(jnp.float32)
     gain_in = gain_all[0:D]
@@ -192,17 +212,6 @@
 
     result, finish_back = jax.vjp(finish_piece, ffn_out, middle, gain_post)
     output = result.astype(jnp.bfloat16)
-    regathered = (
-        lax.all_gather(flat_weights[0], "flat", axis=0, tiled=True),
-        lax.all_gather(flat_weights[1], "flat", axis=0, tiled=True),
-        lax.all_gather(flat_weights[2], "flat", axis=0, tiled=True),
-        lax.all_gather(flat_weights[3], "flat", axis=0, tiled=True),
-        lax.all_gather(flat_weights[4], "flat", axis=0, tiled=True),
-        lax.all_gather(flat_weights[5], "flat", axis=0, tiled=True),
-        lax.all_gather(flat_weights[6], "flat", axis=0, tiled=True),
-        lax.all_gather(flat_weights[7], "flat", axis=0, tiled=True),
-    )
-    mat_query, mat_key, mat_value, mat_out, mat_gate, mat_up, mat_down = unpack(regathered)
     grad_result = cotangent.astype(jnp.float32)
     d_ffn, d_middle_direct, d_gain_post = finish_back(grad_result)
     d_ffn_b = d_ffn.astype(jnp.bfloat16)
@@ -280,16 +289,9 @@
     grad_gains = jnp.concatenate(
         [d_gain_in, d_gain_mid, d_gain_pre, d_gain_post, d_gain_query, d_gain_key]
     )
-    summed = (
-        lax.psum_scatter(grad_query.reshape(-1), "flat", scatter_dimension=0, tiled=True),
-        lax.psum_scatter(grad_key.reshape(-1), "flat", scatter_dimension=0, tiled=True),
-        lax.psum_scatter(grad_value.reshape(-1), "flat", scatter_dimension=0, tiled=True),
-        lax.psum_scatter(grad_out.reshape(-1), "flat", scatter_dimension=0, tiled=True),
-        lax.psum_scatter(grad_gate.reshape(-1), "flat", scatter_dimension=0, tiled=True),
-        lax.psum_scatter(grad_up.reshape(-1), "flat", scatter_dimension=0, tiled=True),
-        lax.psum_scatter(grad_down.reshape(-1), "flat", scatter_dimension=0, tiled=True),
-        lax.psum_scatter(grad_gains, "flat", scatter_dimension=0, tiled=True),
-    )
+    early = scatter_packed((grad_gate, grad_up, grad_down))
+    tail = scatter_packed((grad_query, grad_key, grad_value, grad_out, grad_gains))
+    summed = tail[:4] + early + tail[4:]
     return (
         output,
         grad_in,

time: 834 us -> 597 us (0.72)
  blocking collectives: 166 us -> 0 us
  waiting for transfers between devices: 384 us -> 259 us
  local copies, waits for them, and re-layouts: 89.9 us -> 115 us
  other arithmetic: 33.7 us -> 53.7 us
    unnamed x7 -> x4, waiting for transfers between devices: 319 us -> 0.07 us
    reduce_scatter x0 -> x2, waiting for transfers between devices: none -> 210 us  [scatter_packed(): lax.psum_scatter(joined, 'flat', scatter_dimension=0, tiled=False)]
    all_gather x2 -> x0, blocking collectives: 85.6 us -> none  [the longest x1 44.2 us: per_device(): lax.all_gather(flat_weights[2], 'flat', axis=0, tiled=True)]
    unnamed x2 -> x0, blocking collectives: 80.6 us -> none
    another operation x4 -> x12, local copies, waits for them, and re-layouts: 0.38 us -> 24.9 us  [the longest x1 6.32 us: unpack(): pieces[4].reshape(D, FF)]
    reshape x9 -> x4, local copies, waits for them, and re-layouts: 31.5 us -> 8.44 us  [scatter_packed(): rows = [grad.astype(jnp.bfloat16).reshape(count, -1) for grad in grads]]
    concatenate x0 -> x5, local copies, waits for them, and re-layouts: none -> 17.4 us  [the longest x4 16.8 us: scatter_packed(): packed = jnp.concatenate(rows, axis=1)]
    all_gather x5 -> x2, waiting for transfers between devices: 65.1 us -> 48.8 us  [gather_packed(): joined = lax.all_gather(packed, 'flat', axis=0, tiled=False)]
  transfers between devices with their start and end apart: 12 -> 10, of which waited for: 3 -> 4; matrix products, arithmetic and copies ran while one was open for 18% -> 26% of each run, Pallas kernels for 0% -> 0%
where the time goes in v1:
time: 597 us; the launch traced here: 589 us
  waiting for transfers between devices  259 us (43%)
  matrix products  126 us (21%)
  local copies, waits for them, and re-layouts  115 us (19%)
  other arithmetic  53.7 us (9%)
  between operations  17.4 us (3%)
  starting transfers between devices  17.1 us (3%)
    reduce_scatter x2, waiting for transfers between devices, scatter_packed(): lax.psum_scatter(joined, 'flat', scatter_dimension=0, tiled=False)  210 us
    all_gather x2, waiting for transfers between devices, gather_packed(): joined = lax.all_gather(packed, 'flat', axis=0, tiled=False)  48.8 us
    unnamed x205, local copies, waits for them, and re-layouts  45.8 us
    dot_general x7, matrix products, times_transposed(): lax.dot_general(left, weight, (((1,), (1,)), ((), ())), preferred_element...  32.8 us
    dot_general x7, matrix products, outer_sum(): lax.dot_general(left, right, (((0,), (0,)), ((), ())), preferred_element_...  27.4 us
    dot_general x7, matrix products, forward_dot(): return jnp.dot(left, weight, preferred_element_type=jnp.float32)  21.9 us
    concatenate x4, local copies, waits for them, and re-layouts, scatter_packed(): packed = jnp.concatenate(rows, axis=1)  16.8 us
    ppermute x6, starting transfers between devices, shifted(): return lax.ppermute(block, axis, route)  16.7 us
  transfers between devices with their start and end apart: 10, of which 4 were waited for; matrix products, arithmetic and copies ran while one was open for 26% of the time, Pallas kernels for 0%

profile of v1, /device:TPU:0, one launch (start us, length us, event | category | flops | bytes accessed | tf_op | source)
XLA Modules:
  0.0 588.7 jit_solution(5187982151945575914)
XLA Ops:
  25.3 5.5 collective-permute-start.2
  33.9 40.1 %all-gather.3.cloned.1.call-done = bf16[32,408,128]{2,1,0:T(8,128)(2,1)} async-done(((bf16[1,408,128]{2,1,0:T(8,128)(2,1)}), bf16[32,408,128]{2,1,0:T(8,128)(2,1)}) %all-gather.3.cloned.1.call-update) | async-done | bytes 3342352 | tf_op jit(solution)/shard_map/all_gather | solution.py:78
  111.0 8.0 %fusion.169 = (f32[4,512]{1,0:T(4,128)S(1)}, f32[4,512,1024]{1,2,0:T(8,128)}) fusion(pred[512,1024]{0,1:T(8,128)(4,1)} %get-tuple-element.169, bf16[1024,128]{0,1:T(8,128)(2,1)S(1)} %copy-done.45, bf16[1024,128]{0,1:T(8,128)(2,1)S(1)} %copy-done.47, bf16[1024,4,128]{0,2,1:T(8,128)(2,1)} %get-tuple-element.135, bf16[1024,4,128]{0,2,1:T(8,128)(2,1)S(1)} %get-tuple-element.134), kind=kOutput, calls=%fused_computation.272 | convolution fusion | flops 1085277184 | bytes 11542528 | tf_op jit(solution)/shard_map/sub | solution.py:183
  119.0 5.6 fusion.57
  125.7 8.2 %fusion.174 = (f32[4,512]{1,0:T(4,128)S(1)}, f32[4,512,1024]{1,2,0:T(8,128)}) fusion(pred[512,1024]{0,1:T(8,128)(4,1)} %get-tuple-element.168, bf16[512,256]{0,1:T(8,128)(2,1)} %collective-permute-done.3, bf16[1024,128]{0,1:T(8,128)(2,1)S(1)} %copy-done.45, bf16[1024,128]{0,1:T(8,128)(2,1)S(1)} %copy-done.48, bf16[1024,4,128]{0,2,1:T(8,128)(2,1)} %copy-done.41, ...), kind=kOutput, calls=%fused_computation.273 | convolution fusion | flops 1085801472 | bytes 11804672 | tf_op jit(solution)/shard_map/sub | solution.py:183
  133.9 5.0 fusion.54
  144.9 8.6 %all-gather.5.cloned.1.call-done = bf16[32,960,128]{2,1,0:T(8,128)(2,1)} async-done(((bf16[1,960,128]{2,1,0:T(8,128)(2,1)}), bf16[32,960,128]{2,1,0:T(8,128)(2,1)}) %all-gather.5.cloned.1.call-update) | async-done | bytes 7864336 | tf_op jit(solution)/shard_map/all_gather | solution.py:78
  153.6 11.4 %copy.143 = bf16[4,8,960,128]{3,1,2,0:T(8,128)(2,1)} copy(bf16[4,8,960,128]{3,2,1,0:T(8,128)(2,1)} %bitcast.239) | data formatting | bytes 15728640
  165.0 5.8 fusion.162
  170.8 6.3 %reshape_reshape.25 = bf16[640,2048]{1,0:T(8,128)(2,1)} reshape(bf16[32,40960]{1,0:T(8,128)(2,1)} %get-tuple-element.131) | data formatting | bytes 5242880 | tf_op jit(solution)/shard_map/reshape;reshape | solution.py:69
  177.1 6.3 %reshape_reshape.26 = bf16[640,2048]{1,0:T(8,128)(2,1)} reshape(bf16[32,40960]{1,0:T(8,128)(2,1)} %get-tuple-element.130) | data formatting | bytes 5242880 | tf_op jit(solution)/shard_map/reshape;reshape | solution.py:70
  188.0 5.8 fusion.183
  193.8 8.0 %multiply_convert_fusion.1 = (bf16[1024,2048]{1,0:T(8,128)(2,1)S(1)}, f32[1024,2048]{1,0:T(8,128)}) fusion(f32[1024,2048]{1,0:T(8,128)S(1)} %fusion.183, bf16[1024,640]{0,1:T(8,128)(2,1)S(1)} %copy-done.35, bf16[640,2048]{1,0:T(8,128)(2,1)S(1)} %copy-done.20), kind=kOutput, calls=%fused_computation.24 | convolution fusion | flops 2705326080 | bytes 24903680 | tf_op jit(solution)/shard_map/dot_general | solution.py:56
  208.4 14.6 %multiply_convert_fusion = (bf16[1024,2048]{1,0:T(8,128)(2,1)S(1)}, bf16[1024,2048]{1,0:T(8,128)(2,1)}) fusion(f32[1024,2048]{1,0:T(8,128)} %copy-done.85, f32[1024,2048]{1,0:T(8,128)} %get-tuple-element.183, bf16[1024,640]{0,1:T(8,128)(2,1)S(1)} %get-tuple-element.140, bf16[2048,640]{1,0:T(8,128)(2,1)S(1)} %copy-done.22), kind=kOutput, calls=%fused_computation.23 | convolution fusion | flops 2734686208 | bytes 29097984 | tf_op jit(solution)/shard_map/dot_general | solution.py:50
  223.1 6.7 %fusion.184 = f32[1024,640]{0,1:T(8,128)S(1)} fusion(bf16[1024,2048]{1,0:T(8,128)(2,1)} %get-tuple-element.128, bf16[640,2048]{1,0:T(8,128)(2,1)S(1)} %copy-done.21), kind=kOutput, calls=%fused_computation.275 | convolution fusion | flops 2684354560 | bytes 9437184 | tf_op jit(solution)/shard_map/dot_general | solution.py:50
  315.4 7.3 %convolution_convert_fusion = bf16[2048,640]{1,0:T(8,128)(2,1)} fusion(bf16[1024,2048]{1,0:T(8,128)(2,1)} %copy-done.87, bf16[1024,640]{0,1:T(8,128)(2,1)S(1)} %copy-done.30), kind=kOutput, calls=%fused_computation.63 | convolution fusion | flops 2685665280 | bytes 8126464 | tf_op jit(solution)/shard_map/dot_general | solution.py:44
  322.7 5.6 concatenate.97
  328.3 6.3 %convolution_convert_fusion.2 = bf16[640,2048]{1,0:T(8,128)(2,1)} fusion(bf16[1024,640]{0,1:T(8,128)(2,1)S(1)} %copy-done.36, bf16[1024,2048]{1,0:T(8,128)(2,1)} %get-tuple-element.128), kind=kOutput, calls=%fused_computation.65 | convolution fusion | flops 2685665280 | bytes 8126464 | tf_op jit(solution)/shard_map/dot_general | solution.py:44
  334.6 5.3 concatenate.95
  339.9 6.3 %convolution_convert_fusion.1 = bf16[640,2048]{1,0:T(8,128)(2,1)} fusion(bf16[1024,640]{0,1:T(8,128)(2,1)S(1)} %copy-done.36, bf16[1024,2048]{1,0:T(8,128)(2,1)} %copy-done.86), kind=kOutput, calls=%fused_computation.64 | convolution fusion | flops 2685665280 | bytes 8126464 | tf_op jit(solution)/shard_map/dot_general | solution.py:44
  346.2 5.3 concatenate.96
  351.5 6.7 %pad_maximum_fusion = bf16[32,960,128]{2,1,0:T(8,128)(2,1)} fusion(bf16[32,320,128]{2,1,0:T(8,128)(2,1)} %concatenate.97, bf16[32,320,128]{2,1,0:T(8,128)(2,1)} %concatenate.96, bf16[32,320,128]{2,1,0:T(8,128)(2,1)} %concatenate.95), kind=kLoop, calls=%fused_computation.29 | loop fusion | flops 23592960 | bytes 15728640 | tf_op jit(solution)/shard_map/concatenate | solution.py:91
  365.6 89.5 %reduce-scatter.3.cloned.1.call-done = bf16[1,416,128]{2,1,0:T(8,128)(2,1)} async-done(((bf16[32,416,128]{2,1,0:T(8,128)(2,1)}), bf16[1,416,128]{2,1,0:T(8,128)(2,1)}) %reduce-scatter.3.cloned.1.call-update) | async-done | bytes 106512 | tf_op jit(solution)/shard_map/reduce_scatter | solution.py:93
  459.1 120.9 %reduce-scatter.5.cloned.1.call-done = bf16[1,960,128]{2,1,0:T(8,128)(2,1)} async-done(((bf16[32,960,128]{2,1,0:T(8,128)(2,1)}), bf16[1,960,128]{2,1,0:T(8,128)(2,1)}) %reduce-scatter.5.cloned.1.call-update) | async-done | bytes 245776 | tf_op jit(solution)/shard_map/reduce_scatter | solution.py:93
  (335 shorter events, 172.2 us)
Async XLA Ops:
  7.2 12.2 %copy-start.61 = (s32[1024]{0:T(1024)S(1)}, s32[1024]{0:T(1024)}, u32[]{:S(2)}) copy-start(s32[1024]{0:T(1024)} %param.24) | copy-start | bytes 12292
  7.2 12.8 %copy-start.31 = (bf16[1024,640]{1,0:T(8,128)(2,1)S(1)}, bf16[1024,640]{1,0:T(8,128)(2,1)}, u32[]{:S(2)}) copy-start(bf16[1024,640]{1,0:T(8,128)(2,1)} %param.33) | copy-start | bytes 3932164
  7.2 66.9 %all-gather.3.cloned.1.call-start = ((), (), s32[]{:S(2)}) async-start(), calls=%async_computation.2 | async-start | bytes 3446784 | tf_op jit(solution)/shard_map/all_gather | solution.py:78
  11.7 141.9 %all-gather.5.cloned.1.call-start = ((), (), s32[]{:S(2)}) async-start(), calls=%async_computation.3 | async-start | bytes 8110080 | tf_op jit(solution)/shard_map/all_gather | solution.py:78
  12.5 9.0 %collective-permute-start.1 = (s32[512]{0:T(512)S(1)}, s32[512]{0:T(512)S(1)}, u32[]{:S(2)}, u32[]{:S(2)}) collective-permute-start(s32[512]{0:T(512)S(1)} %get-tuple-element.166), channel_id=1, source_target_pairs={{0,1},{1,2},{2,3},{3,4},{4,5},{5,6},{6,7},{7,8},{8,9},{9,10},{10,1... | collective-permute-start | bytes 6152 | tf_op jit(solution)/shard_map/ppermute | solution.py:20
  16.6 438.6 %reduce-scatter.3.cloned.1.call-start = ((), (), s32[]{:S(2)}) async-start(), calls=%async_computation.4 | async-start | bytes 3514368 | tf_op jit(solution)/shard_map/reduce_scatter | solution.py:93
  19.1 85.9 %copy-start.2 = (bf16[1024,640]{0,1:T(8,128)(2,1)}, bf16[1024,640]{0,1:T(8,128)(2,1)S(1)}, u32[]{:S(2)}) copy-start(bf16[1024,640]{0,1:T(8,128)(2,1)S(1)} %copy.78) | copy-start | bytes 3932164
  19.4 57.1 %copy-start.73 = (f32[1024]{0:T(1024)}, f32[1024]{0:T(1024)S(1)}, u32[]{:S(2)}) copy-start(f32[1024]{0:T(1024)S(1)} %fusion.36) | copy-start | bytes 12292
  19.4 85.6 %copy-start.67 = (f32[1024]{0:T(1024)}, f32[1024]{0:T(1024)S(1)}, u32[]{:S(2)}) copy-start(f32[1024]{0:T(1024)S(1)} %fusion.128) | copy-start | bytes 12292
  19.4 72.4 %copy-start.83 = (f32[128]{0:T(128)}, f32[128]{0:T(128)S(1)}, u32[]{:S(2)}) copy-start(f32[128]{0:T(128)S(1)} %negate_power_fusion) | copy-start | bytes 1540
  25.3 8.0 %collective-permute-start.2 = (s32[1]{0:T(128)}, s32[1]{0:T(128)}, u32[]{:S(2)}, u32[]{:S(2)}) collective-permute-start(s32[1]{0:T(128)} %sub.93), channel_id=1, source_target_pairs={{0,1},{1,2},{2,3},{3,4},{4,5},{5,6},{6,7},{7,8},{8,9},{9,10},{10,1... | collective-permute-start | bytes 20 | tf_op jit(solution)/shard_map/ppermute | solution.py:20
  33.9 57.9 %copy-start.69 = (f32[1024]{0:T(1024)}, f32[1024]{0:T(1024)S(1)}, u32[]{:S(2)}) copy-start(f32[1024]{0:T(1024)S(1)} %fusion.125) | copy-start | bytes 12292
  89.9 17.6 %copy-start.79 = (f32[256]{0:T(256)}, f32[256]{0:T(256)S(1)}, u32[]{:S(2)}) copy-start(f32[256]{0:T(256)S(1)} %get-tuple-element.159) | copy-start | bytes 3076
  90.0 15.0 %copy-start.71 = (f32[640]{0:T(1024)}, f32[640]{0:T(1024)S(1)}, u32[]{:S(2)}) copy-start(f32[640]{0:T(1024)S(1)} %get-tuple-element.158) | copy-start | bytes 7684
  94.9 14.3 %copy-start.15 = (f32[1024,128]{0,1:T(8,128)}, f32[1024,128]{0,1:T(8,128)S(1)}, u32[]{:S(2)}) copy-start(f32[1024,128]{0,1:T(8,128)S(1)} %get-tuple-element.161) | copy-start | bytes 1572868
  95.7 30.0 %collective-permute-start.3 = (bf16[512,256]{0,1:T(8,128)(2,1)}, bf16[512,256]{0,1:T(8,128)(2,1)}, u32[]{:S(2)}, u32[]{:S(2)}) collective-permute-start(bf16[512,256]{0,1:T(8,128)(2,1)} %fusion.102), channel_id=1, source_target_pairs={{0,1},{1,2},{2,3},{3,4},{4,5},{5,6},{6,7},{7,8},{8,9},{9,10},{10,1... | collective-permute-start | bytes 786440 | tf_op jit(solution)/shard_map/ppermute | solution.py:20
  101.5 32.3 %collective-permute-start = (bf16[512,256]{1,0:T(8,128)(2,1)}, bf16[512,256]{1,0:T(8,128)(2,1)}, u32[]{:S(2)}, u32[]{:S(2)}) collective-permute-start(bf16[512,256]{1,0:T(8,128)(2,1)} %slice.341), channel_id=1, source_target_pairs={{0,1},{1,2},{2,3},{3,4},{4,5},{5,6},{6,7},{7,8},{8,9},{9,10},{10,1... | collective-permute-start | bytes 786440 | tf_op jit(solution)/shard_map/ppermute | solution.py:20
  125.6 14.9 %copy-start.32 = (bf16[1024,640]{1,0:T(8,128)(2,1)}, bf16[1024,640]{1,0:T(8,128)(2,1)S(1)}, u32[]{:S(2)}) copy-start(bf16[1024,640]{1,0:T(8,128)(2,1)S(1)} %reshape_reshape.24) | copy-start | bytes 3932164
  208.4 14.6 %copy-start.29 = (bf16[1024,640]{0,1:T(8,128)(2,1)}, bf16[1024,640]{0,1:T(8,128)(2,1)S(1)}, u32[]{:S(2)}) copy-start(bf16[1024,640]{0,1:T(8,128)(2,1)S(1)} %get-tuple-element.140) | copy-start | bytes 3932164
  208.4 14.6 %copy-start.21 = (bf16[640,2048]{1,0:T(8,128)(2,1)S(1)}, bf16[640,2048]{1,0:T(8,128)(2,1)}, u32[]{:S(2)}) copy-start(bf16[640,2048]{1,0:T(8,128)(2,1)} %reshape_reshape.25) | copy-start | bytes 7864324
  236.9 10.4 %slice-start = ((s8[8388608]{0:T(1024)(128)(4,1)}), s8[4194304]{0:T(1024)(128)(4,1)S(1)}, s32[]{:S(2)}) async-start(s8[8388608]{0:T(1024)(128)(4,1)} %bitcast.235), calls=%async_computation.6 | async-start | bytes 8388608
  264.3 28.1 %collective-permute-start.4 = (bf16[512,256]{0,1:T(8,128)(2,1)}, bf16[512,256]{0,1:T(8,128)(2,1)}, u32[]{:S(2)}, u32[]{:S(2)}) collective-permute-start(bf16[512,256]{0,1:T(8,128)(2,1)} %slice.450), channel_id=1, source_target_pairs={{1,0},{2,1},{3,2},{4,3},{5,4},{6,5},{7,6},{8,7},{9,8},{10,9},{11,1... | collective-permute-start | bytes 786440 | tf_op jit(solution)/shard_map/ppermute | solution.py:20
  273.1 24.7 %collective-permute-start.5 = (bf16[512,256]{1,0:T(8,128)(2,1)}, bf16[512,256]{1,0:T(8,128)(2,1)}, u32[]{:S(2)}, u32[]{:S(2)}) collective-permute-start(bf16[512,256]{1,0:T(8,128)(2,1)} %slice.449), channel_id=1, source_target_pairs={{1,0},{2,1},{3,2},{4,3},{5,4},{6,5},{7,6},{8,7},{9,8},{10,9},{11,1... | collective-permute-start | bytes 786440 | tf_op jit(solution)/shard_map/ppermute | solution.py:20
  314.1 265.9 %reduce-scatter.5.cloned.1.call-start = ((), (), s32[]{:S(2)}) async-start(), calls=%async_computation.5 | async-start | bytes 8110080 | tf_op jit(solution)/shard_map/reduce_scatter | solution.py:93
  (78 other events, 264.4 us)
Sparse Core Ops, SparseCore 0:
  11.8 62.2 all-gather.2
  77.0 76.5 all-gather.4
  314.3 140.8 reduce-scatter.2
  461.6 118.3 reduce-scatter.4
